TPU v7x, 512 devices: a whole 4x4x16 slice. The times are simulated.
512 devices in a mesh: freq: 4 (over z_hi), mom: 128 (over y, z_lo, x, core).
Axes of the slice: x: 4, y: 4, z: 16 (z_hi: 4, z_lo: 4; z = z_hi * 4 + z_lo), core: 2. Of those that a mesh axis runs over, the one named last changes fastest.
Arguments:
- vertex: bfloat16 [4, 512, 512, 512], P('freq', 'mom'), may hold values from -6 to 6
- bubble: float32 [4, 512, 512], P('freq', 'mom'), may hold values from 0.0078125 to 0.0625
- mixing: float32 [4, 4], replicated, may hold values from -3 to 3
- lattice_order: int32 [512], replicated, may hold values from 0 to 511, each once
Outputs:
- converted: bfloat16 [4, 512, 256, 512], P('freq', 'mom')
Inputs may be any that keep to these rules, and one draw needn't show every extreme that they name: `lattice_order`: each of the 512 lattice points stands at exactly one index.
All inputs are finite; a program needn't handle non-finite values.
Results may differ from a plain program's by a relative error of at most 0.018.
Values may be sent and summed in bfloat16 or wider, within the bound.
A program may use at most 64 MiB of HBM per device.

v0:
```python
import jax
import jax.numpy as jnp
from jax import lax
from jax.sharding import PartitionSpec as P

LX = 32
LY = 16


def point_table(lattice_order, extent):
    points = jnp.arange(extent, dtype=jnp.int32)
    return (lattice_order[:, None] == points[None, :]).astype(jnp.bfloat16)


def shift_rows(matrix, step_x, step_y):
    extent = matrix.shape[-1]
    lane_y = jnp.arange(extent, dtype=jnp.int32) % LY
    for bit_number in range((LX - 1).bit_length()):
        rolled = jnp.roll(matrix, -(1 << bit_number) * LY, axis=-1)
        matrix = jnp.where(jnp.right_shift(step_x, bit_number) % 2 == 1, rolled, matrix)
    for bit_number in range((LY - 1).bit_length()):
        offset_y = 1 << bit_number
        rolled = jnp.where(
            lane_y + offset_y < LY,
            jnp.roll(matrix, -offset_y, axis=-1),
            jnp.roll(matrix, LY - offset_y, axis=-1),
        )
        matrix = jnp.where(jnp.right_shift(step_y, bit_number) % 2 == 1, rolled, matrix)
    return matrix


def on_device(vertex, bubble, mixing, lattice_order):
    local_freq = vertex.shape[0]
    extent = vertex.shape[2]
    rows_kept = extent // 2
    scaled = (bubble[..., None] * vertex).astype(jnp.bfloat16)
    ladder = (
        vertex + jnp.einsum("wqij,wqjk->wqik", vertex, scaled, preferred_element_type=jnp.float32)
    ).astype(jnp.bfloat16)
    scaled = (bubble[..., None] * ladder).astype(jnp.bfloat16)
    reducible = jnp.einsum(
        "wqij,wqjk->wqik", vertex[:, :, :rows_kept, :], scaled, preferred_element_type=jnp.float32
    ).astype(jnp.bfloat16)
    table = point_table(lattice_order, extent)
    coord_x = (lattice_order // LY)[:rows_kept]
    coord_y = (lattice_order % LY)[:rows_kept]
    by_point = jnp.einsum(
        "wqkc,cP->wqkP", reducible, table, preferred_element_type=jnp.float32
    ).astype(jnp.bfloat16)
    summed = shift_rows(by_point, coord_x[None, None, :, None], coord_y[None, None, :, None])
    outgoing = jnp.einsum(
        "wqkP,pP->wpqk", summed, table, preferred_element_type=jnp.float32
    ).astype(jnp.bfloat16)
    incoming = lax.all_to_all(outgoing, "mom", split_axis=1, concat_axis=2, tiled=True)
    received = jnp.einsum(
        "wpqk,qQ->wpkQ", incoming, table, preferred_element_type=jnp.float32
    ).astype(jnp.bfloat16)
    aligned = shift_rows(
        received, (-coord_x % LX)[None, None, :, None], (-coord_y % LY)[None, None, :, None]
    )
    crossed = jnp.einsum(
        "wpkL,lL->wpkl", aligned, table, preferred_element_type=jnp.float32
    ).astype(jnp.bfloat16)
    own_first = lax.axis_index("freq") * local_freq
    initial = jnp.zeros(crossed.shape, jnp.float32)
    carry = initial
    piece = lax.all_gather(crossed, "freq", axis=0, tiled=True)
    weights = lax.dynamic_slice(mixing, (own_first, 0), (local_freq, piece.shape[0]))
    for member in range(piece.shape[0]):
        carry = carry + weights[:, member][:, None, None, None] * piece[member][None].astype(
            jnp.float32
        )
    return carry.astype(jnp.bfloat16)


def solution(mesh):
    in_specs = (P("freq", "mom", None, None), P("freq", "mom", None), P(), P())
    out_specs = P("freq", "mom", None, None)
    return jax.shard_map(
        on_device, mesh=mesh, in_specs=in_specs, out_specs=out_specs, check_vma=False
    )
```

profile of v0, /device:TPU:1, one launch (start us, length us, event | category | flops | bytes accessed | tf_op | source)
XLA Modules:
  0.0 266.1 jit_solution(3396946909855829190)
XLA Ops:
  6.5 0.7 add_select_fusion.2
  7.3 4.3 %copy.14 = bf16[1,4,512,512]{2,3,1,0:T(8,128)(2,1)} copy(bf16[1,4,512,512]{3,2,1,0:T(8,128)(2,1)} %param.4) | data formatting | bytes 4194304 | tf_op args[0]
  11.6 4.8 %fusion.1 = bf16[1,4,512,512]{2,3,1,0:T(8,128)(2,1)} fusion(bf16[1,4,512,512]{2,3,1,0:T(8,128)(2,1)} %copy.14, bf16[1,4,512,512]{3,2,1,0:T(8,128)(2,1)S(1)} %copy-done.1, f32[4,512]{1,0:T(4,128)S(1)} %bitcast.206), kind=kOutput, calls=%fused_computation.3 | convolution fusion | flops 1080033280 | bytes 6299648 | tf_op jit(solution)/shard_map/wqij,wqjk->wqik/dot_general | solution.py:38
  16.4 3.0 %convolution_convert_fusion.3 = bf16[4,256,512]{2,1,0:T(8,128)(2,1)S(1)} fusion(bf16[1,4,512,512]{2,3,1,0:T(8,128)(2,1)} %fusion.1, f32[4,512]{1,0:T(4,128)S(1)} %bitcast.207, bf16[1,4,512,512]{3,2,1,0:T(8,128)(2,1)S(1)} %copy-done.1, s32[512]{0:T(512)S(1)} %copy-done.2), kind=kOutput, calls=%fused_computation.16 | convolution fusion | flops 1078198272 | bytes 4204544 | tf_op jit(solution)/shard_map/wqkc,cP->wqkP/dot_general | solution.py:47
  19.4 0.4 slice_bitcast_fusion.21
  20.9 0.7 maximum_select_fusion.1
  21.6 0.4 slice_bitcast_fusion.19
  22.6 0.6 maximum_select_fusion.3
  24.3 1.3 fusion.20
  25.8 0.4 slice_bitcast_fusion.16
  26.4 1.2 fusion.21
  27.7 0.5 slice_bitcast_fusion.14
  28.4 1.4 fusion.22
  29.8 0.5 slice_bitcast_fusion.11
  30.5 1.4 fusion.13
  31.8 1.8 copy.17
  33.6 13.8 %all-to-all-start = ((bf16[1,512,4,256]{3,2,0,1:T(4,128)(2,1)}), bf16[1,512,4,256]{3,2,0,1:T(4,128)(2,1)S(1)}, u32[]{:S(2)}, u32[]{:S(2)}) async-start(bf16[1,512,4,256]{3,2,0,1:T(4,128)(2,1)} %copy.17), calls=%async_computation | async-start | bytes 2097152 | tf_op jit(solution)/shard_map/all_to_all | solution.py:54
  47.6 29.5 %all-to-all-done = bf16[1,512,4,256]{3,2,0,1:T(4,128)(2,1)S(1)} async-done(((bf16[1,512,4,256]{3,2,0,1:T(4,128)(2,1)}), bf16[1,512,4,256]{3,2,0,1:T(4,128)(2,1)S(1)}, u32[]{:S(2)}, u32[]{:S(2)}) %all-to-all-start) | async-done | bytes 1048608 | tf_op jit(solution)/shard_map/all_to_all | solution.py:54
  77.4 0.8 convolution_convert_fusion.1
  79.2 0.5 slice_bitcast_fusion.9
  79.7 0.7 maximum_select_fusion.10
  81.4 0.6 maximum_select_fusion.12
  82.5 0.5 slice_bitcast_fusion.7
  83.2 1.4 fusion.30
  84.6 0.5 slice_bitcast_fusion.5
  85.3 1.2 fusion.31
  87.2 1.2 fusion.32
  88.4 0.5 slice_bitcast_fusion
  89.1 2.2 convolution_convert_fusion
  91.4 0.7 fusion.108
  92.0 160.7 %all-gather.3.cloned.1.call-done = bf16[16,256,512]{2,1,0:T(8,128)(2,1)} async-done(((bf16[4,256,512]{2,1,0:T(8,128)(2,1)}), bf16[16,256,512]{2,1,0:T(8,128)(2,1)}) %all-gather.3.cloned.1.call-update) | async-done | bytes 4194320 | tf_op jit(solution)/shard_map/all_gather | solution.py:67
  252.7 6.6 %fusion.19 = bf16[1,4,256,512]{3,2,1,0:T(8,128)(2,1)} fusion(bf16[16,256,512]{2,1,0:T(8,128)(2,1)} %all-gather.3.cloned.1.call-done, f32[]{:T(128)} %bitcast.86, f32[]{:T(128)} %bitcast.85, f32[]{:T(128)} %bitcast.84, f32[]{:T(128)} %bitcast), kind=kLoop, calls=%fused_computation.19 | loop fusion | flops 6291456 | bytes 5242896 | tf_op jit(solution)/shard_map/convert_element_type | solution.py:73
  (62 shorter events, 7.5 us)
Async XLA Ops:
  6.5 84.8 %copy-start = (f32[4,4]{1,0:T(4,128)S(1)}, f32[4,4]{1,0:T(4,128)}, u32[]{:S(2)}) copy-start(f32[4,4]{1,0:T(4,128)} %param.6) | copy-start | bytes 196
  7.2 4.3 %copy-start.1 = (bf16[1,4,512,512]{3,2,1,0:T(8,128)(2,1)S(1)}, bf16[1,4,512,512]{3,2,1,0:T(8,128)(2,1)}, u32[]{:S(2)}) copy-start(bf16[1,4,512,512]{3,2,1,0:T(8,128)(2,1)} %param.4) | copy-start | bytes 6291460
  7.2 4.3 %copy-start.3 = (f32[1,4,512]{2,1,0:T(4,128)S(1)}, f32[1,4,512]{2,1,0:T(4,128)}, u32[]{:S(2)}) copy-start(f32[1,4,512]{2,1,0:T(4,128)} %param.5) | copy-start | bytes 24580
  11.6 4.9 %copy-start.2 = (s32[512]{0:T(512)S(1)}, s32[512]{0:T(512)}, u32[]{:S(2)}) copy-start(s32[512]{0:T(512)} %param.7) | copy-start | bytes 6148
  33.6 43.4 %all-to-all-start = ((bf16[1,512,4,256]{3,2,0,1:T(4,128)(2,1)}), bf16[1,512,4,256]{3,2,0,1:T(4,128)(2,1)S(1)}, u32[]{:S(2)}, u32[]{:S(2)}) async-start(bf16[1,512,4,256]{3,2,0,1:T(4,128)(2,1)} %copy.17), calls=%async_computation | async-start | bytes 2097152 | tf_op jit(solution)/shard_map/all_to_all | solution.py:54
  47.5 205.3 %all-gather.3.cloned.1.call-start = ((), (), s32[]{:S(2)}) async-start(), calls=%async_computation.1 | async-start | bytes 5242880 | tf_op jit(solution)/shard_map/all_gather | solution.py:67
Sparse Core Ops, SparseCore 0:
  91.5 161.2 all-gather.2
where the time goes:
time: 266 us
  waiting for transfers between devices  190 us (71%)
  other arithmetic  19.7 us (7%)
  local copies, waits for them, and re-layouts  16.2 us (6%)
  between operations  14 us (5%)
  starting transfers between devices  13.9 us (5%)
  matrix products  12.2 us (5%)
    all_gather x1, waiting for transfers between devices, on_device(): piece = lax.all_gather(crossed, 'freq', axis=0, tiled=True)  161 us
    all_to_all x1, waiting for transfers between devices, on_device(): lax.all_to_all(outgoing, 'mom', split_axis=1, concat_axis=2, tiled=True)  29.5 us
    all_to_all x1, starting transfers between devices, on_device(): lax.all_to_all(outgoing, 'mom', split_axis=1, concat_axis=2, tiled=True)  13.8 us
    select_n x6, other arithmetic, shift_rows(): jnp.where(jnp.right_shift(step_y, bit_number) % 2 == 1, rolled, matrix)  7.68 us
    convert_element_type x1, other arithmetic, on_device(): return carry.astype(jnp.bfloat16)  6.55 us
  transfers between devices with their start and end apart: 2, of which 2 were waited for; matrix products, arithmetic and copies ran while one was open for 0% of the time, Pallas kernels for 0%

commit v1 on v0

v1 whole, which is shorter than its diff:
```python
import jax
import jax.numpy as jnp
from jax import lax
from jax.experimental import pallas as pl
from jax.experimental.pallas import tpu as pltpu
from jax.sharding import PartitionSpec as P

LX = 32
LY = 16
MESH = pl.DeviceIdType.MESH
F32 = jnp.float32
BF16 = jnp.bfloat16


def dot(a, b, dims=((1,), (0,))):
    return lax.dot_general(a, b, (dims, ((), ())), preferred_element_type=F32)


def iota(shape, axis):
    return lax.broadcasted_iota(jnp.int32, shape, axis)


def one_hot(hit):
    return jnp.where(hit, 1.0, 0.0).astype(BF16)


def zlo_last(r):
    y, xc, zlo, local = r // 128, (r // 16) % 8, (r // 4) % 4, r % 4
    return y * 128 + zlo * 32 + xc * 4 + local


def zlo_second(r):
    y, zlo, xc, local = r // 128, (r // 32) % 4, (r // 4) % 8, r % 4
    return y * 128 + xc * 16 + zlo * 4 + local


def shift_rows(x, kx, ky, sign):
    n = x.shape[-1]
    x = x.reshape(LX, LY, n)
    for bit in range(4):
        rolled = pltpu.roll(x, (-sign * (1 << bit)) % LY, 1)
        x = jnp.where((ky & (1 << bit)) != 0, rolled, x)
    for bit in range(5):
        s = (sign * (1 << bit)) % LX
        rolled = jnp.concatenate([x[s:], x[:s]], axis=0)
        x = jnp.where((kx & (1 << bit)) != 0, rolled, x)
    return x.reshape(LX * LY, n)


def body(v_ref, bub_ref, ord_ref, mix_ref, out_ref,
         tt, ta, tb, tq, pr, pt, da, db, vb, lad, red,
         xa, r1a, ma, r2a, xs, r3, xb, r0, x1, r1b, mb, r2b, dd,
         s1a_s, s1a_r, s2a_s, s2a_r, s3_s, s3_r, s0_s, s0_r, s1b_s, s1b_r, s2b_s, s2b_r):
    f = lax.axis_index("freq")
    m = lax.axis_index("mom")
    core, x, zlo, y = m % 2, (m // 2) % 4, (m // 8) % 4, m // 32
    z = f * 4 + zlo
    here = (y * 4 + x) * 2 + core
    zlo_mix = (zlo + 2) % 4
    slot2 = f * 4 + zlo_mix

    def at_z(freq, low):
        return {"freq": freq, "mom": m - zlo * 8 + low * 8}

    def at_xy(place):
        return {"freq": f, "mom": ((place // 8) * 4 + zlo) * 8 + place % 8}

    barrier = pltpu.get_barrier_semaphore()

    def greet_z(i, _):
        t = (z + i) % 16
        pl.semaphore_signal(barrier, inc=1, device_id=at_z(t // 4, t % 4), device_id_type=MESH)
        return _

    def greet_xy(i, _):
        pl.semaphore_signal(barrier, inc=1, device_id=at_xy((here + i) % 32), device_id_type=MESH)
        return _

    lax.fori_loop(1, 16, greet_z, 0)
    lax.fori_loop(1, 32, greet_xy, 0)

    order = ord_ref[...]
    kx = order[:, :256] // LY
    ky = order[:, :256] % LY
    tt[...] = one_hot(iota((512, 512), 0) == order)
    for b in range(4):
        column = jnp.transpose(jnp.broadcast_to(order[:, b * 128:(b + 1) * 128], (128, 128)))
        for c in range(4):
            ta[b * 128:(b + 1) * 128, c * 128:(c + 1) * 128] = one_hot(
                column == iota((128, 128), 1) + c * 128)
    pr[...] = one_hot(zlo_last(iota((512, 1), 0)) == iota((1, 512), 1))
    tb[...] = dot(pr[...], ta[...]).astype(BF16)

    def send1(src, dst, ssem, rsem, ql, go):
        for j in range(4):
            cp = pltpu.make_async_remote_copy(
                src.at[ql, j], dst.at[ql, f], ssem.at[ql], rsem.at[ql],
                device_id=at_z(j, zlo_mix), device_id_type=MESH)
            cp.start()

    def compute(ql, carry):
        bub = bub_ref[pl.ds(ql, 1), :]
        vb[...] = (v_ref[ql].astype(F32) * bub).astype(BF16)
        for h in range(2):
            rows = pl.ds(h * 256, 256)
            lad[rows, :] = (v_ref[ql, rows, :].astype(F32) + dot(vb[rows, :], v_ref[ql])).astype(BF16)
        red[...] = dot(vb[:256, :], lad[...]).astype(BF16)
        moved = []
        for h in range(2):
            lanes = slice(h * 128, (h + 1) * 128)
            point = dot(tt[...], red[lanes, :], ((1,), (1,)))
            moved.append(shift_rows(point, kx[:, lanes], ky[:, lanes], 1).astype(BF16))
        xa[ql] = dot(ta[...], moved[0]).astype(BF16).reshape(4, 128, 128)
        xb[:, pl.ds(ql, 1)] = dot(tb[...], moved[1]).astype(BF16).reshape(32, 1, 16, 128)

        @pl.when(ql == 0)
        def _():
            pl.semaphore_wait(barrier, 46)

        send1(xa, r1a, s1a_s, s1a_r, ql, None)
        return carry

    lax.fori_loop(0, 4, compute, 0)

    def spread(src, dst, ssem, rsem):
        pltpu.make_async_copy(src.at[here], dst.at[here], rsem).start()

        def one(i, _):
            to = (here + i) % 32
            pltpu.make_async_remote_copy(
                src.at[to], dst.at[here], ssem, rsem, device_id=at_xy(to), device_id_type=MESH).start()
            return _

        lax.fori_loop(1, 32, one, 0)

    def send2(src, dst, ssem, rsem):
        pltpu.make_async_copy(src.at[f, zlo], dst.at[slot2], rsem).start()

        def one(i, _):
            t = (z + i) % 16
            pltpu.make_async_remote_copy(
                src.at[t // 4, t % 4], dst.at[slot2], ssem, rsem,
                device_id=at_z(t // 4, t % 4), device_id_type=MESH).start()
            return _

        lax.fori_loop(1, 16, one, 0)

    def got(ref, sem):
        pltpu.make_async_copy(ref, ref, sem).wait()

    def mix(src, dst, ssem, rsem, ql):
        got(src.at[ql], rsem.at[ql])
        parts = [src[ql, b].astype(F32) for b in range(4)]
        for a in range(4):
            total = mix_ref[a, 0] * parts[0]
            for b in range(1, 4):
                total = total + mix_ref[a, b] * parts[b]
            dst[ql, a] = total.astype(BF16).reshape(4, 32, 128)

    def mix_a(ql, _):
        mix(r1a, ma, s1a_s, s1a_r, ql)
        send2(ma.at[ql], r2a.at[ql], s2a_s.at[ql], s2a_r.at[ql])
        return _

    def mix_b(ql, _):
        mix(r1b, mb, s1b_s, s1b_r, ql)
        send2(mb.at[ql], r2b.at[ql], s2b_s.at[ql], s2b_r.at[ql])
        return _

    spread(xb, r0, s0_s, s0_r)
    pt[...] = one_hot(zlo_second(iota((512, 1), 0)) == iota((1, 512), 1))
    row, col = iota((512, 1), 0), iota((1, 512), 1)
    db[...] = one_hot((row % 128) * 4 + row // 128 == col)
    da[...] = one_hot(zlo_second((row % 128) * 4 + row // 128) == col)
    tq[...] = dot(tt[...], db[...], ((1,), (1,))).astype(BF16)

    lax.fori_loop(0, 2, mix_a, 0)
    got(r0, s0_r)

    def first_b(ql, _):
        rows = r0[:, pl.ds(ql, 1)].reshape(512, 128)
        x1[ql] = dot(pt[...], rows).astype(BF16).reshape(4, 128, 128)
        send1(x1, r1b, s1b_s, s1b_r, ql, None)
        return _

    lax.fori_loop(0, 4, first_b, 0)
    lax.fori_loop(2, 4, mix_a, 0)

    def third_a(ql, _):
        got(r2a.at[ql], s2a_r.at[ql])
        xs[ql] = dot(pr[...], r2a[ql].reshape(512, 128)).astype(BF16).reshape(32, 16, 128)
        spread(xs.at[ql], r3.at[ql], s3_s.at[ql], s3_r.at[ql])
        return mix_b(ql, _)

    lax.fori_loop(0, 4, third_a, 0)

    def finish(h):
        lanes = slice(h * 128, (h + 1) * 128)

        def one(local, _):
            g = dot(tq[...], dd[h, local].reshape(512, 128))
            moved = jnp.transpose(shift_rows(g, kx[:, lanes], ky[:, lanes], -1)).astype(BF16)
            out_ref[local, lanes, :] = dot(moved, tt[...]).astype(BF16)
            return _

        lax.fori_loop(0, 4, one, 0)

    def last_a(ql, _):
        got(r3.at[ql], s3_r.at[ql])
        rows = dot(da[...], r3[ql].reshape(512, 128)).astype(BF16)
        dd[0, :, pl.ds(ql, 1)] = rows.reshape(4, 1, 128, 128)
        return _

    def last_b(ql, _):
        got(r2b.at[ql], s2b_r.at[ql])
        rows = dot(db[...], r2b[ql].reshape(512, 128)).astype(BF16)
        dd[1, :, pl.ds(ql, 1)] = rows.reshape(4, 1, 128, 128)
        return _

    lax.fori_loop(0, 4, last_a, 0)
    finish(0)
    lax.fori_loop(0, 4, last_b, 0)
    finish(1)

    def drain(ql, _):
        got(xa.at[ql], s1a_s.at[ql])
        got(x1.at[ql], s1b_s.at[ql])
        for s in (s2a_s, s2b_s):
            pltpu.make_async_copy(ma.at[ql, pl.ds(0, 3)], ma.at[ql, pl.ds(0, 3)], s.at[ql]).wait()
            pltpu.make_async_copy(ma.at[ql, 0, pl.ds(0, 3)], ma.at[ql, 0, pl.ds(0, 3)], s.at[ql]).wait()
        got(xs.at[ql, pl.ds(0, 31)], s3_s.at[ql])
        return _

    lax.fori_loop(0, 4, drain, 0)
    got(xb.at[pl.ds(0, 31)], s0_s)


def on_device(vertex, bubble, mixing, lattice_order):
    def vm(*shape):
        return pltpu.VMEM(shape, BF16)

    sem = pltpu.SemaphoreType.DMA
    out = pl.pallas_call(
        body,
        out_shape=jax.ShapeDtypeStruct((4, 256, 512), BF16),
        in_specs=[pl.BlockSpec(memory_space=pltpu.VMEM)] * 3 + [pl.BlockSpec(memory_space=pltpu.SMEM)],
        out_specs=pl.BlockSpec(memory_space=pltpu.VMEM),
        scratch_shapes=[
            vm(512, 512), vm(512, 512), vm(512, 512), vm(512, 512),
            vm(512, 512), vm(512, 512), vm(512, 512), vm(512, 512),
            vm(512, 512), vm(512, 512), vm(256, 512),
            vm(4, 4, 128, 128), vm(4, 4, 128, 128), vm(4, 4, 4, 32, 128), vm(4, 16, 32, 128),
            vm(4, 32, 16, 128), vm(4, 32, 16, 128),
            vm(32, 4, 16, 128), vm(32, 4, 16, 128),
            vm(4, 4, 128, 128), vm(4, 4, 128, 128), vm(4, 4, 4, 32, 128), vm(4, 16, 32, 128),
            vm(2, 4, 4, 128, 128),
            sem((4,)), sem((4,)), sem((4,)), sem((4,)), sem((4,)), sem((4,)),
            sem, sem, sem((4,)), sem((4,)), sem((4,)), sem((4,)),
        ],
        compiler_params=pltpu.CompilerParams(
            collective_id=1, has_side_effects=True, vmem_limit_bytes=40 * 2**20),
        cost_estimate=pl.CostEstimate(flops=4 * 10**9, bytes_accessed=4 * 2**20, transcendentals=0),
    )(vertex[0], bubble[0], lattice_order.reshape(1, 512), mixing)
    return out[None]


def solution(mesh):
    in_specs = (P("freq", "mom", None, None), P("freq", "mom", None), P(), P())
    out_specs = P("freq", "mom", None, None)
    return jax.shard_map(
        on_device, mesh=mesh, in_specs=in_specs, out_specs=out_specs, check_vma=False
    )
```

time: 266 us -> 121 us (0.45)
  waiting for transfers between devices: 190 us -> 0 us
  Pallas kernels: 0 us -> 116 us
  other arithmetic: 19.7 us -> 0 us
  between operations: 14 us -> 0.01 us
  starting transfers between devices: 13.9 us -> 0 us
  matrix products: 12.2 us -> 0 us
  local copies, waits for them, and re-layouts: 16.2 us -> 4.62 us
    all_gather x1 -> x0, waiting for transfers between devices: 161 us -> none  [on_device(): piece = lax.all_gather(crossed, 'freq', axis=0, tiled=True)]
    pallas_call x0 -> x1, Pallas kernels: none -> 116 us  [on_device(): pl.pallas_call(body, out_shape=jax.ShapeDtypeStruct((4, 256, 512), BF16),...]
    all_to_all x1 -> x0, waiting for transfers between devices: 29.5 us -> none  [on_device(): lax.all_to_all(outgoing, 'mom', split_axis=1, concat_axis=2, tiled=True)]
    all_to_all x1 -> x0, starting transfers between devices: 13.8 us -> none  [on_device(): lax.all_to_all(outgoing, 'mom', split_axis=1, concat_axis=2, tiled=True)]
    select_n x17 -> x0, other arithmetic: 13.1 us -> none  [the longest x6 7.68 us: shift_rows(): jnp.where(jnp.right_shift(step_y, bit_number) % 2 == 1, rolled, matrix)]
    dot_general x5 -> x0, matrix products: 12.2 us -> none  [the longest x1 4.85 us: on_device(): jnp.einsum('wqij,wqjk->wqik', vertex, scaled, preferred_element_type=jnp....]
    concatenate x46 -> x0, local copies, waits for them, and re-layouts: 8.95 us -> none  [the longest x18 3.37 us: shift_rows(): rolled = jnp.roll(matrix, -(1 << bit_number) * LY, axis=-1)]
    convert_element_type x1 -> x0, other arithmetic: 6.55 us -> none  [on_device(): return carry.astype(jnp.bfloat16)]
  transfers between devices with their start and end apart: 2 -> 0, of which waited for: 2 -> 0; matrix products, arithmetic and copies ran while one was open for 0% -> 0% of each run, Pallas kernels for 0% -> 0%
where the time goes in v1:
time: 121 us
  Pallas kernels  116 us (96%)
  local copies, waits for them, and re-layouts  4.62 us (4%)
    pallas_call x1, Pallas kernels, on_device(): pl.pallas_call(body, out_shape=jax.ShapeDtypeStruct((4, 256, 512), BF16),...  116 us
    unnamed x9, local copies, waits for them, and re-layouts  4.62 us

profile of v1, /device:TPU:1, one launch (start us, length us, event | category | flops | bytes accessed | tf_op | source)
XLA Modules:
  0.0 120.6 jit_solution(6882923957251125208)
XLA Ops:
  0.0 0.0 copy-start
  0.0 1.6 %copy-done = bf16[1,4,512,512]{3,2,1,0:T(8,128)(2,1)S(1)} copy-done((bf16[1,4,512,512]{3,2,1,0:T(8,128)(2,1)S(1)}, bf16[1,4,512,512]{3,2,1,0:T(8,128)(2,1)}, u32[]{:S(2)}) %copy-start) | copy-done | bytes 2097176
  1.6 0.0 copy-start.1
  1.6 0.7 copy-done.1
  2.3 0.0 copy-start.2
  2.3 0.7 copy-done.2
  3.0 0.0 copy-start.3
  3.0 0.7 copy-done.3
  3.7 116.0 %shard_map.46 = bf16[4,256,512]{2,1,0:T(8,128)(2,1)S(1)} custom-call(bf16[4,512,512]{2,1,0:T(8,128)(2,1)S(1)} %bitcast.5, f32[4,512]{1,0:T(4,128)S(1)} %bitcast.6, s32[1,512]{1,0:T(1,128)S(1)} %bitcast.7, f32[4,4]{1,0:T(4,128)S(1)} %copy-done.3), custom_call_target="tpu_custom_call" | custom-call | flops 4000000000 | bytes 4194304 | tf_op jit(solution)/shard_map/pallas_call | solution.py:243
  119.6 1.0 copy.6
Async XLA Ops:
  0.0 1.6 %copy-start = (bf16[1,4,512,512]{3,2,1,0:T(8,128)(2,1)S(1)}, bf16[1,4,512,512]{3,2,1,0:T(8,128)(2,1)}, u32[]{:S(2)}) copy-start(bf16[1,4,512,512]{3,2,1,0:T(8,128)(2,1)} %param.4) | copy-start | bytes 6291460
  1.6 0.7 copy-start.1
  2.3 0.7 copy-start.2
  3.0 0.7 copy-start.3

commit v2 on v1

v2 whole, which is shorter than its diff:
```python
import jax
import jax.numpy as jnp
from jax import lax
from jax.experimental import pallas as pl
from jax.experimental.pallas import tpu as pltpu
from jax.sharding import PartitionSpec as P

LX = 32
LY = 16
MESH = pl.DeviceIdType.MESH
F32 = jnp.float32
BF16 = jnp.bfloat16


def dot(a, b, dims=((1,), (0,))):
    return lax.dot_general(a, b, (dims, ((), ())), preferred_element_type=F32)


def iota(shape, axis):
    return lax.broadcasted_iota(jnp.int32, shape, axis)


def one_hot(hit):
    return jnp.where(hit, 1.0, 0.0).astype(BF16)


def zlo_last(r):
    y, xc, zlo, local = r // 128, (r // 16) % 8, (r // 4) % 4, r % 4
    return y * 128 + zlo * 32 + xc * 4 + local


def zlo_second(r):
    y, zlo, xc, local = r // 128, (r // 32) % 4, (r // 4) % 8, r % 4
    return y * 128 + xc * 16 + zlo * 4 + local


def shift_rows(x, kx, ky, sign):
    n = x.shape[-1]
    x = x.reshape(LX, LY, n)
    for bit in range(4):
        rolled = pltpu.roll(x, (-sign * (1 << bit)) % LY, 1)
        x = jnp.where((ky & (1 << bit)) != 0, rolled, x)
    for bit in range(5):
        s = (sign * (1 << bit)) % LX
        rolled = jnp.concatenate([x[s:], x[:s]], axis=0)
        x = jnp.where((kx & (1 << bit)) != 0, rolled, x)
    return x.reshape(LX * LY, n)


def body(v_hbm, bub_hbm, ord_hbm, mix_hbm, out_hbm,
         v_ref, bub_ref, ord_ref, mix_ref, out_ref,
         tt, ta, tb, tq, pr, pt, da, qq, vb, lad, red,
         xa, r1a, ma, r2a, xs, r3, xb, r0, mid, x1, r1b, mb, r2b, dd,
         in_s, out_s, s1a_s, s1a_r, s2a_s, s2a_r, s3_s, s3_r, s0_s, s0_r, s1b_s, s1b_r, s2b_s, s2b_r):
    f = lax.axis_index("freq")
    m = lax.axis_index("mom")
    core, x, zlo, y = m % 2, (m // 2) % 4, (m // 8) % 4, m // 32
    z = f * 4 + zlo
    here = (y * 4 + x) * 2 + core
    zlo_mix = (zlo + 2) % 4
    slot2 = f * 4 + zlo_mix

    def at_z(freq, low):
        return {"freq": freq, "mom": m - zlo * 8 + low * 8}

    def at_xy(place):
        return {"freq": f, "mom": ((place // 8) * 4 + zlo) * 8 + place % 8}

    loads = [pltpu.make_async_copy(v_hbm.at[q], v_ref.at[q], in_s.at[q]) for q in range(4)]
    loads += [
        pltpu.make_async_copy(a, b, in_s.at[4 + i])
        for i, (a, b) in enumerate(((bub_hbm, bub_ref), (ord_hbm, ord_ref), (mix_hbm, mix_ref)))
    ]
    for i in (0, 4, 5, 1, 2, 3, 6):
        loads[i].start()

    barrier = pltpu.get_barrier_semaphore()

    def greet_z(i, _):
        t = (z + i) % 16
        pl.semaphore_signal(barrier, inc=1, device_id=at_z(t // 4, t % 4), device_id_type=MESH)
        return _

    def greet_xy(i, _):
        pl.semaphore_signal(barrier, inc=1, device_id=at_xy((here + i) % 32), device_id_type=MESH)
        return _

    lax.fori_loop(1, 16, greet_z, 0)
    lax.fori_loop(1, 32, greet_xy, 0)

    def got(ref, sem):
        pltpu.make_async_copy(ref, ref, sem).wait()

    def send1(src, dst, ssem, rsem):
        for j in range(4):
            pltpu.make_async_remote_copy(
                src.at[j], dst.at[f], ssem, rsem,
                device_id=at_z(j, zlo_mix), device_id_type=MESH).start()

    def spread(src, dst, ssem, rsem):
        pltpu.make_async_copy(src.at[here], dst.at[here], rsem).start()

        def one(i, _):
            to = (here + i) % 32
            pltpu.make_async_remote_copy(
                src.at[to], dst.at[here], ssem, rsem, device_id=at_xy(to), device_id_type=MESH).start()
            return _

        lax.fori_loop(1, 32, one, 0)

    def send2(src, dst, ssem, rsem):
        pltpu.make_async_copy(src.at[f, zlo], dst.at[slot2], rsem).start()

        def one(i, _):
            near = (i + 1) // 2
            t = (z + 8 + near - 2 * near * (i % 2)) % 16
            pltpu.make_async_remote_copy(
                src.at[t // 4, t % 4], dst.at[slot2], ssem, rsem,
                device_id=at_z(t // 4, t % 4), device_id_type=MESH).start()
            return _

        lax.fori_loop(0, 15, one, 0)

    def ladder(ql):
        bub = bub_ref[pl.ds(ql, 1), :]
        vb[...] = (v_ref[ql].astype(F32) * bub).astype(BF16)
        for h in range(2):
            rows = pl.ds(h * 256, 256)
            lad[rows, :] = (v_ref[ql, rows, :].astype(F32) + dot(vb[rows, :], v_ref[ql])).astype(BF16)
        red[ql] = dot(vb[:256, :], lad[...]).astype(BF16)

    def coords(h):
        order = ord_ref[:, h * 128:(h + 1) * 128]
        return order // LY, order % LY

    def to_transfer(ql, h, rows):
        point = dot(tt[...], red[ql, h * 128:(h + 1) * 128, :], ((1,), (1,)))
        return dot(rows[...], shift_rows(point, *coords(h), 1).astype(BF16)).astype(BF16)

    def first_a(ql):
        xa[ql] = to_transfer(ql, 0, ta).reshape(4, 128, 128)

    for i in (0, 4, 5):
        loads[i].wait()
    ladder(0)
    order = ord_ref[...]
    tt[...] = one_hot(iota((512, 512), 0) == order)
    for b in range(4):
        column = jnp.transpose(jnp.broadcast_to(order[:, b * 128:(b + 1) * 128], (128, 128)))
        for c in range(4):
            ta[b * 128:(b + 1) * 128, c * 128:(c + 1) * 128] = one_hot(
                column == iota((128, 128), 1) + c * 128)
    first_a(0)
    pl.semaphore_wait(barrier, 46)
    send1(xa.at[0], r1a.at[0], s1a_s.at[0], s1a_r.at[0])
    for i in (1, 2, 3, 6):
        loads[i].wait()

    def more_a(ql, _):
        ladder(ql)
        first_a(ql)
        send1(xa.at[ql], r1a.at[ql], s1a_s.at[ql], s1a_r.at[ql])
        return _

    lax.fori_loop(1, 4, more_a, 0)

    pr[...] = one_hot(zlo_last(iota((512, 1), 0)) == iota((1, 512), 1))
    tb[...] = dot(pr[...], ta[...]).astype(BF16)

    def first_b(ql, _):
        xb[:, pl.ds(ql, 1)] = to_transfer(ql, 1, tb).reshape(32, 1, 16, 128)
        return _

    lax.fori_loop(0, 4, first_b, 0)
    spread(xb, r0, s0_s, s0_r)

    row, col = iota((512, 1), 0), iota((1, 512), 1)
    pt[...] = one_hot(zlo_second(row) == col)
    da[...] = one_hot(zlo_second((row % 128) * 4 + row // 128) == col)
    tq[...] = dot(tt[...], one_hot((row % 128) * 4 + row // 128 == col), ((1,), (1,))).astype(BF16)
    r64 = iota((256, 1), 0)
    qq[...] = one_hot(
        (r64 // 64) * 64 + (r64 % 4) * 16 + ((r64 // 4) % 4) * 4 + (r64 // 16) % 4 == iota((1, 256), 1))

    def mix(src, dst, rsem):
        got(src, rsem)
        parts = [src[b].astype(F32) for b in range(4)]
        for a in range(4):
            total = mix_ref[a, 0] * parts[0]
            for b in range(1, 4):
                total = total + mix_ref[a, b] * parts[b]
            dst[a] = total.astype(BF16).reshape(4, 32, 128)

    def mix_a(ql, _):
        mix(r1a.at[ql], ma.at[ql], s1a_r.at[ql])
        send2(ma.at[ql], r2a.at[ql], s2a_s.at[ql], s2a_r.at[ql])
        return _

    def mix_b(local, _):
        mix(r1b.at[local], mb.at[local], s1b_r.at[local])
        send2(mb.at[local], r2b.at[local], s2b_s.at[local], s2b_r.at[local])
        return _

    lax.fori_loop(0, 2, mix_a, 0)
    got(r0, s0_r)
    for i in range(8):
        rows = r0[i * 4:(i + 1) * 4].reshape(256, 128)
        rows = dot(qq[...], rows).astype(BF16).reshape(4, 4, 16, 128)
        for local in range(4):
            mid[local, i * 4:(i + 1) * 4] = rows[:, local]

    def second_b(local, _):
        x1[local] = dot(pt[...], mid[local].reshape(512, 128)).astype(BF16).reshape(4, 128, 128)
        send1(x1.at[local], r1b.at[local], s1b_s.at[local], s1b_r.at[local])
        return _

    lax.fori_loop(0, 4, second_b, 0)
    lax.fori_loop(2, 4, mix_a, 0)

    def third_a(ql, _):
        got(r2a.at[ql], s2a_r.at[ql])
        xs[ql] = dot(pr[...], r2a[ql].reshape(512, 128)).astype(BF16).reshape(32, 16, 128)
        spread(xs.at[ql], r3.at[ql], s3_s.at[ql], s3_r.at[ql])
        return mix_b(ql, _)

    lax.fori_loop(0, 4, third_a, 0)

    def finish(h, local, table, rows):
        point = dot(table[...], rows.reshape(512, 128))
        moved = jnp.transpose(shift_rows(point, *coords(h), -1)).astype(BF16)
        lines = pl.ds(h * 128, 128)
        out_ref[local, lines, :] = dot(moved, tt[...]).astype(BF16)
        pltpu.make_async_copy(out_ref.at[local, lines], out_hbm.at[local, lines], out_s).start()

    def last_a(ql, _):
        got(r3.at[ql], s3_r.at[ql])
        rows = dot(da[...], r3[ql].reshape(512, 128)).astype(BF16)
        dd[:, pl.ds(ql, 1)] = rows.reshape(4, 1, 128, 128)
        return _

    def finish_a(local, _):
        finish(0, local, tq, dd[local])
        return _

    def finish_b(local, _):
        got(r2b.at[local], s2b_r.at[local])
        finish(1, local, tt, r2b[local])
        return _

    lax.fori_loop(0, 4, last_a, 0)
    lax.fori_loop(0, 4, finish_a, 0)
    lax.fori_loop(0, 4, finish_b, 0)

    def drain(i, _):
        got(xa.at[i], s1a_s.at[i])
        got(x1.at[i], s1b_s.at[i])
        for s in (s2a_s, s2b_s):
            got(ma.at[i, pl.ds(0, 3)], s.at[i])
            got(ma.at[i, 0, pl.ds(0, 3)], s.at[i])
        got(xs.at[i, pl.ds(0, 31)], s3_s.at[i])
        return _

    lax.fori_loop(0, 4, drain, 0)
    got(xb.at[pl.ds(0, 31)], s0_s)
    got(out_ref, out_s)


def on_device(vertex, bubble, mixing, lattice_order):
    def vm(*shape):
        return pltpu.VMEM(shape, BF16)

    sem = pltpu.SemaphoreType.DMA
    out = pl.pallas_call(
        body,
        out_shape=jax.ShapeDtypeStruct((4, 256, 512), BF16),
        in_specs=[pl.BlockSpec(memory_space=pl.ANY)] * 4,
        out_specs=pl.BlockSpec(memory_space=pl.ANY),
        scratch_shapes=[
            vm(4, 512, 512), pltpu.VMEM((4, 512), F32), pltpu.VMEM((1, 512), jnp.int32),
            pltpu.SMEM((4, 4), F32), vm(4, 256, 512),
            vm(512, 512), vm(512, 512), vm(512, 512), vm(512, 512),
            vm(512, 512), vm(512, 512), vm(512, 512), vm(256, 256),
            vm(512, 512), vm(512, 512), vm(4, 256, 512),
            vm(4, 4, 128, 128), vm(4, 4, 128, 128), vm(4, 4, 4, 32, 128), vm(4, 16, 32, 128),
            vm(4, 32, 16, 128), vm(4, 32, 16, 128),
            vm(32, 4, 16, 128), vm(32, 4, 16, 128), vm(4, 32, 16, 128),
            vm(4, 4, 128, 128), vm(4, 4, 128, 128), vm(4, 4, 4, 32, 128), vm(4, 16, 32, 128),
            vm(4, 4, 128, 128),
            sem((7,)), sem, sem((4,)), sem((4,)), sem((4,)), sem((4,)), sem((4,)), sem((4,)),
            sem, sem, sem((4,)), sem((4,)), sem((4,)), sem((4,)),
        ],
        compiler_params=pltpu.CompilerParams(
            collective_id=1, has_side_effects=True, vmem_limit_bytes=56 * 2**20),
        cost_estimate=pl.CostEstimate(flops=4 * 10**9, bytes_accessed=4 * 2**20, transcendentals=0),
    )(vertex[0], bubble[0], lattice_order.reshape(1, 512), mixing)
    return out[None]


def solution(mesh):
    in_specs = (P("freq", "mom", None, None), P("freq", "mom", None), P(), P())
    out_specs = P("freq", "mom", None, None)
    return jax.shard_map(
        on_device, mesh=mesh, in_specs=in_specs, out_specs=out_specs, check_vma=False
    )
```

time: 121 us -> 113 us (0.934)
  Pallas kernels: 116 us -> 110 us
  local copies, waits for them, and re-layouts: 4.62 us -> 2.26 us
    pallas_call x1, Pallas kernels: 116 us -> 110 us  [on_device(): pl.pallas_call(body, out_shape=jax.ShapeDtypeStruct((4, 256, 512), BF16),...]
    unnamed x9 -> x1, local copies, waits for them, and re-layouts: 4.62 us -> 2.26 us
where the time goes in v2:
time: 113 us
  Pallas kernels  110 us (97%)
  local copies, waits for them, and re-layouts  2.26 us (2%)
    pallas_call x1, Pallas kernels, on_device(): pl.pallas_call(body, out_shape=jax.ShapeDtypeStruct((4, 256, 512), BF16),...  110 us
    unnamed x1, local copies, waits for them, and re-layouts  2.26 us

profile of v2, /device:TPU:1, one launch (start us, length us, event | category | flops | bytes accessed | tf_op | source)
XLA Modules:
  0.0 112.8 jit_solution(5636162588489752126)
XLA Ops:
  0.0 110.5 %shard_map.46 = bf16[4,256,512]{2,1,0:T(8,128)(2,1)} custom-call(bf16[4,512,512]{2,1,0:T(8,128)(2,1)} %bitcast.5, f32[4,512]{1,0:T(4,128)} %bitcast.6, s32[1,512]{1,0:T(1,128)} %bitcast.7, f32[4,4]{1,0:T(4,128)} %mix_hbm.1), custom_call_target="tpu_custom_call" | custom-call | flops 4000000000 | bytes 4194304 | tf_op jit(solution)/shard_map/pallas_call | solution.py:273
  110.5 2.3 %copy.6 = bf16[1,4,256,512]{3,2,1,0:T(8,128)(2,1)} copy(bf16[1,4,256,512]{3,2,1,0:T(8,128)(2,1)} %bitcast.4) | data formatting | bytes 2097152

commit v3 on v2

--- a/solution.py
+++ b/solution.py
@@ -47,8 +47,8 @@
     return x.reshape(LX * LY, n)
 
 
-def body(v_hbm, bub_hbm, ord_hbm, mix_hbm, out_hbm,
-         v_ref, bub_ref, ord_ref, mix_ref, out_ref,
+def body(v_hbm, bub_hbm, ord_hbm, mix_hbm, out_ref,
+         v_ref, bub_ref, ord_ref, mix_ref,
          tt, ta, tb, tq, pr, pt, da, qq, vb, lad, red,
          xa, r1a, ma, r2a, xs, r3, xb, r0, mid, x1, r1b, mb, r2b, dd,
          in_s, out_s, s1a_s, s1a_r, s2a_s, s2a_r, s3_s, s3_r, s0_s, s0_r, s1b_s, s1b_r, s2b_s, s2b_r):
@@ -118,6 +118,21 @@
                 src.at[t // 4, t % 4], dst.at[slot2], ssem, rsem,
                 device_id=at_z(t // 4, t % 4), device_id_type=MESH).start()
             return _
+
+        lax.fori_loop(0, 15, one, 0)
+
+    def send2_some(ql, first):
+        def one(i, carry):
+            near = (i + 1) // 2
+            t = (z + 8 + near - 2 * near * (i % 2)) % 16
+
+            @pl.when(t < 4 if first else t >= 4)
+            def _():
+                pltpu.make_async_remote_copy(
+                    mb.at[ql, t // 4, t % 4], r2b.at[ql, slot2], s2b_s.at[ql], s2b_r.at[ql],
+                    device_id=at_z(t // 4, t % 4), device_id_type=MESH).start()
+
+            return carry
 
         lax.fori_loop(0, 15, one, 0)
 
@@ -198,7 +213,13 @@
 
     def mix_b(local, _):
         mix(r1b.at[local], mb.at[local], s1b_r.at[local])
-        send2(mb.at[local], r2b.at[local], s2b_s.at[local], s2b_r.at[local])
+        pltpu.make_async_copy(mb.at[local, f, zlo], r2b.at[local, slot2], s2b_r.at[local]).start()
+        send2_some(local, True)
+
+        @pl.when(local > 0)
+        def _late():
+            send2_some(local - 1, False)
+
         return _
 
     lax.fori_loop(0, 2, mix_a, 0)
@@ -224,13 +245,13 @@
         return mix_b(ql, _)
 
     lax.fori_loop(0, 4, third_a, 0)
+    send2_some(3, False)
 
     def finish(h, local, table, rows):
         point = dot(table[...], rows.reshape(512, 128))
         moved = jnp.transpose(shift_rows(point, *coords(h), -1)).astype(BF16)
         lines = pl.ds(h * 128, 128)
         out_ref[local, lines, :] = dot(moved, tt[...]).astype(BF16)
-        pltpu.make_async_copy(out_ref.at[local, lines], out_hbm.at[local, lines], out_s).start()
 
     def last_a(ql, _):
         got(r3.at[ql], s3_r.at[ql])
@@ -262,7 +283,6 @@
 
     lax.fori_loop(0, 4, drain, 0)
     got(xb.at[pl.ds(0, 31)], s0_s)
-    got(out_ref, out_s)
 
 
 def on_device(vertex, bubble, mixing, lattice_order):
@@ -272,12 +292,12 @@
     sem = pltpu.SemaphoreType.DMA
     out = pl.pallas_call(
         body,
-        out_shape=jax.ShapeDtypeStruct((4, 256, 512), BF16),
+        out_shape=pltpu.VMEM((4, 256, 512), BF16),
         in_specs=[pl.BlockSpec(memory_space=pl.ANY)] * 4,
-        out_specs=pl.BlockSpec(memory_space=pl.ANY),
+        out_specs=pl.BlockSpec(memory_space=pltpu.VMEM),
         scratch_shapes=[
             vm(4, 512, 512), pltpu.VMEM((4, 512), F32), pltpu.VMEM((1, 512), jnp.int32),
-            pltpu.SMEM((4, 4), F32), vm(4, 256, 512),
+            pltpu.SMEM((4, 4), F32),
             vm(512, 512), vm(512, 512), vm(512, 512), vm(512, 512),
             vm(512, 512), vm(512, 512), vm(512, 512), vm(256, 256),
             vm(512, 512), vm(512, 512), vm(4, 256, 512),

time: 113 us -> 108 us (0.956); the launches traced: 113 us -> 106 us
  Pallas kernels: 110 us -> 105 us
  local copies, waits for them, and re-layouts: 2.26 us -> 0.97 us
    pallas_call x1, Pallas kernels: 110 us -> 105 us  [on_device(): pl.pallas_call(body, out_shape=pltpu.VMEM((4, 256, 512), BF16), in_specs=...]
    unnamed x1, local copies, waits for them, and re-layouts: 2.26 us -> 0.97 us
where the time goes in v3:
time: 108 us; the launch traced here: 106 us
  Pallas kernels  105 us (97%)
    pallas_call x1, Pallas kernels, on_device(): pl.pallas_call(body, out_shape=pltpu.VMEM((4, 256, 512), BF16), in_specs=...  105 us

profile of v3, /device:TPU:1, one launch (start us, length us, event | category | flops | bytes accessed | tf_op | source)
XLA Modules:
  0.0 106.5 jit_solution(9016431821156343838)
XLA Ops:
  0.0 105.5 %shard_map.46 = bf16[4,256,512]{2,1,0:T(8,128)(2,1)S(1)} custom-call(bf16[4,512,512]{2,1,0:T(8,128)(2,1)} %bitcast.5, f32[4,512]{1,0:T(4,128)} %bitcast.6, s32[1,512]{1,0:T(1,128)} %bitcast.7, f32[4,4]{1,0:T(4,128)} %mix_hbm.1), custom_call_target="tpu_custom_call" | custom-call | flops 4000000000 | bytes 4194304 | tf_op jit(solution)/shard_map/pallas_call | solution.py:293
  105.5 1.0 copy.6

commit v4 on v3

--- a/solution.py
+++ b/solution.py
@@ -51,7 +51,7 @@
          v_ref, bub_ref, ord_ref, mix_ref,
          tt, ta, tb, tq, pr, pt, da, qq, vb, lad, red,
          xa, r1a, ma, r2a, xs, r3, xb, r0, mid, x1, r1b, mb, r2b, dd,
-         in_s, out_s, s1a_s, s1a_r, s2a_s, s2a_r, s3_s, s3_r, s0_s, s0_r, s1b_s, s1b_r, s2b_s, s2b_r):
+         sides_s, rows_s, in_s, s1a_s, s1a_r, s2a_s, s2a_r, s3_s, s3_r, s0_s, s0_r, s1b_s, s1b_r, s2b_s, s2b_r):
     f = lax.axis_index("freq")
     m = lax.axis_index("mom")
     core, x, zlo, y = m % 2, (m // 2) % 4, (m // 8) % 4, m // 32
@@ -66,6 +66,20 @@
     def at_xy(place):
         return {"freq": f, "mom": ((place // 8) * 4 + zlo) * 8 + place % 8}
 
+    def greet(semaphore, device):
+        pl.semaphore_signal(semaphore, inc=1, device_id=device, device_id_type=MESH)
+
+    barrier = pltpu.get_barrier_semaphore()
+    row = m % 8
+    z_sides = [at_z(((z + d) % 16) // 4, (zlo + d) % 4) for d in (1, 15)]
+    other_rows = [{"freq": f, "mom": (m + 32 * d) % 128} for d in range(1, 4)]
+    for j in range(4):
+        greet(barrier, at_z(j, zlo_mix))
+    for device in z_sides + other_rows:
+        greet(barrier, device)
+    for d in range(1, 8):
+        greet(barrier, {"freq": f, "mom": m - row + (row + d) % 8})
+
     loads = [pltpu.make_async_copy(v_hbm.at[q], v_ref.at[q], in_s.at[q]) for q in range(4)]
     loads += [
         pltpu.make_async_copy(a, b, in_s.at[4 + i])
@@ -73,20 +87,6 @@
     ]
     for i in (0, 4, 5, 1, 2, 3, 6):
         loads[i].start()
-
-    barrier = pltpu.get_barrier_semaphore()
-
-    def greet_z(i, _):
-        t = (z + i) % 16
-        pl.semaphore_signal(barrier, inc=1, device_id=at_z(t // 4, t % 4), device_id_type=MESH)
-        return _
-
-    def greet_xy(i, _):
-        pl.semaphore_signal(barrier, inc=1, device_id=at_xy((here + i) % 32), device_id_type=MESH)
-        return _
-
-    lax.fori_loop(1, 16, greet_z, 0)
-    lax.fori_loop(1, 32, greet_xy, 0)
 
     def got(ref, sem):
         pltpu.make_async_copy(ref, ref, sem).wait()
@@ -166,7 +166,11 @@
             ta[b * 128:(b + 1) * 128, c * 128:(c + 1) * 128] = one_hot(
                 column == iota((128, 128), 1) + c * 128)
     first_a(0)
-    pl.semaphore_wait(barrier, 46)
+    pl.semaphore_wait(barrier, 16)
+    for device in z_sides:
+        greet(sides_s, device)
+    for device in other_rows:
+        greet(rows_s, device)
     send1(xa.at[0], r1a.at[0], s1a_s.at[0], s1a_r.at[0])
     for i in (1, 2, 3, 6):
         loads[i].wait()
@@ -187,12 +191,13 @@
         return _
 
     lax.fori_loop(0, 4, first_b, 0)
+    pl.semaphore_wait(rows_s, 3)
     spread(xb, r0, s0_s, s0_r)
 
-    row, col = iota((512, 1), 0), iota((1, 512), 1)
-    pt[...] = one_hot(zlo_second(row) == col)
-    da[...] = one_hot(zlo_second((row % 128) * 4 + row // 128) == col)
-    tq[...] = dot(tt[...], one_hot((row % 128) * 4 + row // 128 == col), ((1,), (1,))).astype(BF16)
+    line, col = iota((512, 1), 0), iota((1, 512), 1)
+    pt[...] = one_hot(zlo_second(line) == col)
+    da[...] = one_hot(zlo_second((line % 128) * 4 + line // 128) == col)
+    tq[...] = dot(tt[...], one_hot((line % 128) * 4 + line // 128 == col), ((1,), (1,))).astype(BF16)
     r64 = iota((256, 1), 0)
     qq[...] = one_hot(
         (r64 // 64) * 64 + (r64 % 4) * 16 + ((r64 // 4) % 4) * 4 + (r64 // 16) % 4 == iota((1, 256), 1))
@@ -222,7 +227,6 @@
 
         return _
 
-    lax.fori_loop(0, 2, mix_a, 0)
     got(r0, s0_r)
     for i in range(8):
         rows = r0[i * 4:(i + 1) * 4].reshape(256, 128)
@@ -236,7 +240,8 @@
         return _
 
     lax.fori_loop(0, 4, second_b, 0)
-    lax.fori_loop(2, 4, mix_a, 0)
+    pl.semaphore_wait(sides_s, 2)
+    lax.fori_loop(0, 4, mix_a, 0)
 
     def third_a(ql, _):
         got(r2a.at[ql], s2a_r.at[ql])
@@ -306,7 +311,8 @@
             vm(32, 4, 16, 128), vm(32, 4, 16, 128), vm(4, 32, 16, 128),
             vm(4, 4, 128, 128), vm(4, 4, 128, 128), vm(4, 4, 4, 32, 128), vm(4, 16, 32, 128),
             vm(4, 4, 128, 128),
-            sem((7,)), sem, sem((4,)), sem((4,)), sem((4,)), sem((4,)), sem((4,)), sem((4,)),
+            pltpu.SemaphoreType.REGULAR, pltpu.SemaphoreType.REGULAR,
+            sem((7,)), sem((4,)), sem((4,)), sem((4,)), sem((4,)), sem((4,)), sem((4,)),
             sem, sem, sem((4,)), sem((4,)), sem((4,)), sem((4,)),
         ],
         compiler_params=pltpu.CompilerParams(

time: 108 us -> 106 us (0.981); the launches traced: 106 us -> 106 us
  no operation moved by 1% of the time
where the time goes in v4:
time: 106 us
  Pallas kernels  105 us (99%)
    pallas_call x1, Pallas kernels, on_device(): pl.pallas_call(body, out_shape=pltpu.VMEM((4, 256, 512), BF16), in_specs=...  105 us

profile of v4, /device:TPU:1, one launch (start us, length us, event | category | flops | bytes accessed | tf_op | source)
XLA Modules:
  0.0 105.6 jit_solution(18403081410577600515)
XLA Ops:
  0.0 104.7 %shard_map.46 = bf16[4,256,512]{2,1,0:T(8,128)(2,1)S(1)} custom-call(bf16[4,512,512]{2,1,0:T(8,128)(2,1)} %bitcast.5, f32[4,512]{1,0:T(4,128)} %bitcast.6, s32[1,512]{1,0:T(1,128)} %bitcast.7, f32[4,4]{1,0:T(4,128)} %mix_hbm.1), custom_call_target="tpu_custom_call" | custom-call | flops 4000000000 | bytes 4194304 | tf_op jit(solution)/shard_map/pallas_call | solution.py:298
  104.7 1.0 copy.6

commit v5 on v4

--- a/solution.py
+++ b/solution.py
@@ -227,6 +227,8 @@
 
         return _
 
+    pl.semaphore_wait(sides_s, 2)
+    lax.fori_loop(0, 1 * core, mix_a, 0)
     got(r0, s0_r)
     for i in range(8):
         rows = r0[i * 4:(i + 1) * 4].reshape(256, 128)
@@ -240,8 +242,7 @@
         return _
 
     lax.fori_loop(0, 4, second_b, 0)
-    pl.semaphore_wait(sides_s, 2)
-    lax.fori_loop(0, 4, mix_a, 0)
+    lax.fori_loop(1 * core, 4, mix_a, 0)
 
     def third_a(ql, _):
         got(r2a.at[ql], s2a_r.at[ql])

time: 106 us -> 106 us (level); the launches traced: 106 us -> 105 us
    pallas_call x1, Pallas kernels: 105 us -> 104 us  [on_device(): pl.pallas_call(body, out_shape=pltpu.VMEM((4, 256, 512), BF16), in_specs=...]
where the time goes in v5:
time: 106 us; the launch traced here: 105 us
  Pallas kernels  104 us (98%)
    pallas_call x1, Pallas kernels, on_device(): pl.pallas_call(body, out_shape=pltpu.VMEM((4, 256, 512), BF16), in_specs=...  104 us

profile of v5, /device:TPU:1, one launch (start us, length us, event | category | flops | bytes accessed | tf_op | source)
XLA Modules:
  0.0 104.5 jit_solution(13918621084851343265)
XLA Ops:
  0.0 103.6 %shard_map.46 = bf16[4,256,512]{2,1,0:T(8,128)(2,1)S(1)} custom-call(bf16[4,512,512]{2,1,0:T(8,128)(2,1)} %bitcast.5, f32[4,512]{1,0:T(4,128)} %bitcast.6, s32[1,512]{1,0:T(1,128)} %bitcast.7, f32[4,4]{1,0:T(4,128)} %mix_hbm.1), custom_call_target="tpu_custom_call" | custom-call | flops 4000000000 | bytes 4194304 | tf_op jit(solution)/shard_map/pallas_call | solution.py:299
  103.6 1.0 copy.6

commit v6 on v5

--- a/solution.py
+++ b/solution.py
@@ -221,9 +221,9 @@
         pltpu.make_async_copy(mb.at[local, f, zlo], r2b.at[local, slot2], s2b_r.at[local]).start()
         send2_some(local, True)
 
-        @pl.when(local > 0)
+        @pl.when(local + core > 1)
         def _late():
-            send2_some(local - 1, False)
+            send2_some(local + core - 2, False)
 
         return _
 
@@ -251,6 +251,11 @@
         return mix_b(ql, _)
 
     lax.fori_loop(0, 4, third_a, 0)
+
+    @pl.when(core == 0)
+    def _last():
+        send2_some(2, False)
+
     send2_some(3, False)
 
     def finish(h, local, table, rows):

time: 106 us -> 106 us (level)
  no operation moved by 1% of the time
where the time goes in v6:
time: 106 us
  Pallas kernels  105 us (99%)
    pallas_call x1, Pallas kernels, on_device(): pl.pallas_call(body, out_shape=pltpu.VMEM((4, 256, 512), BF16), in_specs=...  105 us

profile of v6, /device:TPU:1, one launch (start us, length us, event | category | flops | bytes accessed | tf_op | source)
XLA Modules:
  0.0 105.6 jit_solution(11838539971607697630)
XLA Ops:
  0.0 104.6 %shard_map.46 = bf16[4,256,512]{2,1,0:T(8,128)(2,1)S(1)} custom-call(bf16[4,512,512]{2,1,0:T(8,128)(2,1)} %bitcast.5, f32[4,512]{1,0:T(4,128)} %bitcast.6, s32[1,512]{1,0:T(1,128)} %bitcast.7, f32[4,4]{1,0:T(4,128)} %mix_hbm.1), custom_call_target="tpu_custom_call" | custom-call | flops 4000000000 | bytes 4194304 | tf_op jit(solution)/shard_map/pallas_call | solution.py:304
  104.6 1.0 copy.6
